TPU v7x, 128 devices: a whole 4x4x4 slice. The times are simulated.
128 devices in a mesh: row: 16 (over x_lo, z, core), col: 8 (over x_hi, y).
Axes of the slice: x: 4 (x_hi: 2, x_lo: 2; x = x_hi * 2 + x_lo), y: 4, z: 4, core: 2. Of those that a mesh axis runs over, the one named last changes fastest.
Arguments:
- atom_pos: float32 [2, 3, 16384], P(None, None, ('row', 'col')), may hold values from -5 to 5
- noise: float32 [2, 3, 16384], P(None, None, ('row', 'col')), may hold values from -5 to 5
- noise_level: float32 [2], replicated, may hold values from 0.25 to 4
- atom_single: bfloat16 [16384, 128], P(('row', 'col')), may hold values from -21 to 21
- w_pos: float32 [3, 128], replicated, may hold values from -3.5 to 3.5
- atom_bias: bfloat16 [4, 16384, 128], P(None, ('row', 'col')), may hold values from -4 to 250
- atom_qkv: bfloat16 [128, 384], replicated, may hold values from -0.5 to 0.5
- atom_out: bfloat16 [128, 128], replicated, may hold values from -0.5 to 0.5
- w_agg: bfloat16 [128, 768], replicated, may hold values from -0.5 to 0.5
- atom_token: int32 [16384], P(('row', 'col')), may hold values from 0 to 2047, as said below
- token_counts: int32 [2048], P(('row', 'col')), may hold values from 2 to 24, as said below
- pair: bfloat16 [2048, 2048, 128], P('row', 'col'), may hold values from -82 to 82
- w_pairbias: bfloat16 [128, 32], replicated, may hold values from -4 to 4
- tok_proj: bfloat16 [2, 768, 3072], replicated, may hold values from -0.21875 to 0.21875
- tok_out: bfloat16 [2, 768, 768], replicated, may hold values from -0.21875 to 0.21875
- w_dec: bfloat16 [768, 128], replicated, may hold values from -0.21875 to 0.21875
- w_update: bfloat16 [128, 3], replicated, may hold values from -0.5 to 0.5
Outputs:
- denoised: float32 [2, 3, 16384], P(None, None, ('row', 'col'))
Inputs may be any that keep to these rules, and one draw needn't show every extreme that they name: `atom_token`: nondecreasing along the atoms; the atoms of device index d along row+col (atoms d*128 to d*128 + 127) belong to tokens (d-1)*16 to (d+1)*16 - 1, those of device 0 to tokens below 16. token_counts[n] is the number of atoms a with atom_token[a] = n.
All inputs are finite; a program needn't handle non-finite values.
Results may differ from a plain program's by a relative error of at most 0.01005.
Values may be sent and summed in bfloat16 or wider, within the bound.
A program may use at most 128 MiB of HBM per device.

v0:
```python
import math

import jax
import jax.numpy as jnp
from jax import lax
from jax.experimental import pallas as pl
from jax.experimental.pallas import tpu as pltpu
from jax.sharding import PartitionSpec as P

HEADS = 16
HEAD = 48
D_TOK = 768
HEADS_A = 4
HEAD_A = 32
C_ATOM = 128
Q_WIN = 32
K_WIN = 128
MARGIN = 48
BLOCKS = 2
SAMPLES = 2
TOK_DEV = 16
A_DEV = 128
ROWS = 16
COLS = 8
DEVICES = ROWS * COLS
QUERIES = COLS * TOK_DEV
KEYS = ROWS * TOK_DEV
PART = D_TOK + 128
STRIDE = QUERIES + 8
LN_EPSILON = 1e-05
LOG2E = math.log2(math.e)
MESH = pl.DeviceIdType.MESH
F32 = jnp.float32
BF16 = jnp.bfloat16

HEAD_TILES = ((0, 1), (0, 1), (0, 2), (1, 1), (1, 1), (1, 2), (2, 1), (2, 1))


def dot(a, b, dims=((1,), (0,)), precision=None):
    return lax.dot_general(
        a, b, (dims, ((), ())), precision=precision, preferred_element_type=F32
    )


def iota(shape, dim):
    return lax.broadcasted_iota(jnp.int32, shape, dim)


def layer_norm(v):
    mean = jnp.mean(v, axis=-1, keepdims=True)
    centred = v - mean
    var = jnp.mean(centred * centred, axis=-1, keepdims=True)
    return centred * lax.rsqrt(var + LN_EPSILON)


def swap2(i):
    return i + 2 - 4 * lax.rem(lax.div(i, 2), 2)


def kernel(
    noise_level_hbm,
    atom_pos_hbm,
    noise_hbm,
    atom_single_hbm,
    w_pos_hbm,
    atom_bias_hbm,
    atom_qkv_hbm,
    atom_out_hbm,
    w_agg_hbm,
    atom_token_hbm,
    token_counts_hbm,
    pair_hbm,
    w_pairbias_hbm,
    tok_proj_hbm,
    tok_out_hbm,
    w_dec_hbm,
    w_update_hbm,
    out,
    noise_level,
    atom_pos,
    noise,
    atom_single,
    w_pos,
    atom_bias,
    atom_qkv,
    atom_out,
    w_agg,
    atom_token,
    token_counts,
    w_pairbias,
    w_dec,
    w_update,
    pair,
    proj,
    tok_out,
    bias,
    w_spread,
    centre,
    expand,
    atom_enc,
    queries_a,
    kv_own,
    halo,
    kv_pad,
    spill_out,
    spill_in,
    token_act,
    gates,
    q_all,
    kv_all,
    q_ref,
    k_ref,
    v_ref,
    stat,
    part,
    part_in,
    dec_out,
    dec_in,
    input_sem,
    pair_sem,
    weight_sem,
    halo_send,
    halo_recv,
    spill_sems,
    dec_sems,
    turn_send,
    turn_recv,
    q_send,
    q_recv,
    kv_send,
    kv_recv,
    twin_send,
    twin_recv,
    part_send,
    part_recv,
):
    r = lax.axis_index("row")
    c = lax.axis_index("col")
    d = r * COLS + c
    up = lax.rem(d + 1, DEVICES)
    down = lax.rem(d + DEVICES - 1, DEVICES)
    up_id = (lax.div(up, COLS), lax.rem(up, COLS))
    down_id = (lax.div(down, COLS), lax.rem(down, COLS))
    core = lax.rem(r, 2)
    level_r = lax.div(r, 2)
    twin_id = (r + 1 - 2 * core, c)
    turn_to = (2 * swap2(c) + core, level_r)
    turn_from = (2 * c + core, swap2(level_r))
    slot = core * COLS + swap2(level_r)
    turn_slot = core * COLS + c

    barrier = pltpu.get_barrier_semaphore()

    def greet(device):
        pl.semaphore_signal(barrier, inc=1, device_id=device, device_id_type=MESH)

    def each(first, last, act):
        def step(j, _):
            act(j)
            return 0

        lax.fori_loop(first, last, step, 0)

    greet(turn_from)
    greet(up_id)
    greet(down_id)
    each(1, COLS, lambda j: greet((r, lax.rem(c + j, COLS))))
    each(1, ROWS // 2, lambda j: greet((lax.rem(r + 2 * j, ROWS), c)))
    greet(twin_id)

    small = [
        (noise_level_hbm, noise_level),
        (atom_pos_hbm, atom_pos),
        (noise_hbm, noise),
        (atom_single_hbm, atom_single),
        (w_pos_hbm, w_pos),
        (atom_qkv_hbm, atom_qkv),
        (w_pairbias_hbm, w_pairbias),
        (atom_bias_hbm, atom_bias),
        (atom_out_hbm, atom_out),
        (w_agg_hbm, w_agg),
        (atom_token_hbm, atom_token),
        (token_counts_hbm, token_counts),
        (w_dec_hbm, w_dec),
        (w_update_hbm, w_update),
    ]
    small_copies = [
        pltpu.make_async_copy(a, b, input_sem.at[i]) for i, (a, b) in enumerate(small)
    ]
    for copy in small_copies:
        copy.start()

    def pair_copy(i):
        rows = pl.ds(i * 32, 32)
        return pltpu.make_async_copy(pair_hbm.at[rows], pair.at[rows], pair_sem.at[i])

    proj_copies = [
        pltpu.make_async_copy(tok_proj_hbm.at[b], proj.at[b], weight_sem.at[b]) for b in range(2)
    ]
    out_copies = [
        pltpu.make_async_copy(tok_out_hbm.at[b], tok_out.at[b], weight_sem.at[2 + b])
        for b in range(2)
    ]
    for i in range(4):
        pair_copy(i).start()
    for b in range(2):
        proj_copies[b].start()
        out_copies[b].start()
    for copy in small_copies[:7]:
        copy.wait()

    row_i, col_i = iota((KEYS, KEYS), 0), iota((KEYS, KEYS), 1)
    same = row_i // C_ATOM == col_i // C_ATOM
    centre[...] = (
        jnp.where(row_i == col_i, 1.0, 0.0) - jnp.where(same, 1.0 / C_ATOM, 0.0)
    ).astype(BF16)
    heads_wide = iota((2 * HEADS, KEYS), 1) // 8 == iota((2 * HEADS, KEYS), 0)
    wide = dot(w_pairbias[...], jnp.where(heads_wide, 1.0, 0.0).astype(BF16), ((0,), (0,)))
    query_of = lax.rem(iota((C_ATOM, KEYS), 1), 8)
    for q in range(8):
        w_spread[q * C_ATOM : (q + 1) * C_ATOM, :] = jnp.where(query_of == q, wide, 0.0).astype(
            BF16
        )

    def pair_bias(first, last):
        def step(i, _):
            q0 = pl.multiple_of(i * 8, 8)
            centred, squares = [], []
            for p in range(4):
                two = jnp.concatenate([pair[q0 + 2 * p], pair[q0 + 2 * p + 1]], axis=1)
                part_centred = dot(two, centre[...])
                centred.append(part_centred.astype(BF16))
                squares.append(part_centred * part_centred)
            y = dot(jnp.concatenate(centred, axis=1), w_spread[...])
            query = lax.rem(iota((KEYS, C_ATOM), 1), 8)
            total = jnp.zeros((KEYS, C_ATOM), F32)
            for q in range(8):
                half = slice((q % 2) * C_ATOM, (q % 2 + 1) * C_ATOM)
                mine = jnp.sum(squares[q // 2][:, half], axis=1, keepdims=True)
                total = jnp.where(query == q, mine, total)
            scale = lax.rsqrt(total * (1.0 / C_ATOM) + LN_EPSILON) * LOG2E
            turned = (y * jnp.concatenate([scale, scale], axis=1)).T
            for t in range(KEYS // 128):
                for h in range(2 * HEADS):
                    bias[t, pl.ds(pl.multiple_of(h * STRIDE + q0, 8), 8), :] = turned[
                        h * 8 : (h + 1) * 8, t * 128 : (t + 1) * 128
                    ]
            return 0

        lax.fori_loop(first, last, step, 0)

    acts = []
    for s in range(SAMPLES):
        level = jnp.broadcast_to(noise_level[:, s : s + 1], (1, A_DEV))
        noisy = atom_pos[:, s] + level * noise[:, s]
        scaled = noisy / jnp.sqrt(level * level + 1.0)
        acts.append(
            atom_single[...].astype(F32)
            + dot(scaled, w_pos[...], ((0,), (0,)), lax.Precision.HIGHEST)
        )
    act = jnp.concatenate(acts, axis=0)
    atom_enc[...] = act
    projected = dot(layer_norm(act).astype(BF16), atom_qkv[...]).astype(BF16)
    for s in range(SAMPLES):
        rows = slice(s * A_DEV, (s + 1) * A_DEV)
        queries_a[s] = projected[rows, 0:C_ATOM]
        kv_own[s] = projected[rows, C_ATOM:]
    pl.semaphore_wait(barrier, 1 + 2 + (COLS - 1) + (ROWS // 2 - 1) + 1)

    def halo_copies():
        return (
            pltpu.make_async_remote_copy(
                src_ref=kv_own.at[:, pl.ds(A_DEV - MARGIN, MARGIN)],
                dst_ref=halo.at[0],
                send_sem=halo_send.at[0],
                recv_sem=halo_recv.at[0],
                device_id=up_id,
                device_id_type=MESH,
            ),
            pltpu.make_async_remote_copy(
                src_ref=kv_own.at[:, pl.ds(0, MARGIN)],
                dst_ref=halo.at[1],
                send_sem=halo_send.at[1],
                recv_sem=halo_recv.at[1],
                device_id=down_id,
                device_id_type=MESH,
            ),
        )

    to_up, to_down = halo_copies()
    to_up.start()
    to_down.start()
    for i in range(4):
        pair_copy(i).wait()
    pair_bias(0, 6)
    for copy in small_copies[7:]:
        copy.wait()
    to_up.wait()
    to_down.wait()
    for s in range(SAMPLES):
        kv_pad[s, 0:MARGIN] = halo[0, s]
        kv_pad[s, MARGIN : MARGIN + A_DEV] = kv_own[s]
        kv_pad[s, MARGIN + A_DEV : A_DEV + 2 * MARGIN] = halo[1, s]

    lane_head = iota((HEADS_A, Q_WIN, C_ATOM), 2) // HEAD_A == iota((HEADS_A, Q_WIN, C_ATOM), 0)
    head_mask = jnp.where(lane_head, 1.0, 0.0)
    head_mask_low = head_mask.astype(BF16)
    slots = iota((1, K_WIN), 1)
    for s in range(SAMPLES):
        mixed = []
        for w in range(A_DEV // Q_WIN):
            rows = slice(w * Q_WIN, (w + 1) * Q_WIN)
            window = slice(w * Q_WIN, w * Q_WIN + K_WIN)
            query = (queries_a[s, rows][None] * head_mask_low).reshape(HEADS_A * Q_WIN, C_ATOM)
            score = dot(query, kv_pad[s, window, 0:C_ATOM], ((1,), (1,))) * (1 / math.sqrt(HEAD_A))
            score = score + atom_bias[:, rows, :].astype(F32).reshape(HEADS_A * Q_WIN, K_WIN)
            index = d * A_DEV + w * Q_WIN - MARGIN + slots
            inside = (index >= 0) & (index < DEVICES * A_DEV)
            score = jnp.where(inside, score, -1e30)
            p = jnp.exp(score - jnp.max(score, axis=-1, keepdims=True))
            total = jnp.sum(p, axis=-1, keepdims=True)
            mix = dot(p.astype(BF16), kv_pad[s, window, C_ATOM:]) / total
            mixed.append(
                jnp.sum(mix.reshape(HEADS_A, Q_WIN, C_ATOM) * head_mask, axis=0)
            )
        rows = slice(s * A_DEV, (s + 1) * A_DEV)
        mix = jnp.concatenate(mixed, axis=0).astype(BF16)
        atom_enc[rows] = atom_enc[rows] + dot(mix, atom_out[...])

    slot_index = atom_token[...] - (d * TOK_DEV - TOK_DEV)
    member = jnp.where(
        slot_index == iota((2 * TOK_DEV, A_DEV), 0), 1.0, 0.0
    )
    member_low = member.astype(BF16)
    hidden = jnp.maximum(dot(atom_enc[...].astype(BF16), w_agg[...]), 0.0)
    for s in range(SAMPLES):
        mine = hidden[s * A_DEV : (s + 1) * A_DEV]
        high = mine.astype(BF16)
        low = (mine - high.astype(F32)).astype(BF16)
        sums = dot(
            jnp.concatenate([member_low, member_low], axis=1),
            jnp.concatenate([high, low], axis=0),
        )
        spill_out[s] = sums[0:TOK_DEV].astype(BF16)
        token_act[s] = sums[TOK_DEV : 2 * TOK_DEV]
    spill = pltpu.make_async_remote_copy(
        src_ref=spill_out,
        dst_ref=spill_in,
        send_sem=spill_sems.at[0],
        recv_sem=spill_sems.at[1],
        device_id=down_id,
        device_id_type=MESH,
    )
    spill.start()
    pair_bias(6, 11)
    lanes = iota((D_TOK, 2 * C_ATOM), 0)
    head_of = lax.rem(iota((D_TOK, 2 * C_ATOM), 1), C_ATOM)
    expand[...] = jnp.where(
        (lanes >= head_of * HEAD) & (lanes < head_of * HEAD + HEAD), 1.0, 0.0
    ).astype(BF16)
    diagonal = iota((TOK_DEV, TOK_DEV), 0) == iota((TOK_DEV, TOK_DEV), 1)
    counts = jnp.sum(
        jnp.where(diagonal, token_counts[...].astype(F32), 0.0), axis=1, keepdims=True
    )
    spill.wait()
    for s in range(SAMPLES):
        token_act[s] = (token_act[s] + spill_in[s].astype(F32)) / counts

    def q_copy(b, s, j):
        return pltpu.make_async_remote_copy(
            src_ref=q_all.at[b, s, c],
            dst_ref=q_all.at[b, s, c],
            send_sem=q_send.at[b, s, j],
            recv_sem=q_recv.at[b, s, c],
            device_id=(r, lax.rem(c + j, COLS)),
            device_id_type=MESH,
        )

    def q_arrival(b, s, j):
        peer = lax.rem(c + j, COLS)
        return pltpu.make_async_remote_copy(
            src_ref=q_all.at[b, s, peer],
            dst_ref=q_all.at[b, s, peer],
            send_sem=q_send.at[b, s, j],
            recv_sem=q_recv.at[b, s, peer],
            device_id=(r, peer),
            device_id_type=MESH,
        )

    def turn_copy(b, s):
        return pltpu.make_async_remote_copy(
            src_ref=q_all.at[b, s, c],
            dst_ref=kv_all.at[b, s, turn_slot],
            send_sem=turn_send.at[b, s],
            recv_sem=turn_recv.at[b, s],
            device_id=turn_to,
            device_id_type=MESH,
        )

    def turn_arrival(b, s):
        return pltpu.make_async_remote_copy(
            src_ref=q_all.at[b, s, c],
            dst_ref=kv_all.at[b, s, slot],
            send_sem=turn_send.at[b, s],
            recv_sem=turn_recv.at[b, s],
            device_id=turn_from,
            device_id_type=MESH,
        )

    def kv_copy(b, s, j):
        return pltpu.make_async_remote_copy(
            src_ref=kv_all.at[b, s, slot],
            dst_ref=kv_all.at[b, s, slot],
            send_sem=kv_send.at[b, s, j],
            recv_sem=kv_recv.at[b, s, level_r],
            device_id=(lax.rem(r + 2 * j, ROWS), c),
            device_id_type=MESH,
        )

    def kv_arrival(b, s, j):
        peer = lax.rem(r + 2 * j, ROWS)
        peer_slot = core * COLS + swap2(lax.div(peer, 2))
        return pltpu.make_async_remote_copy(
            src_ref=kv_all.at[b, s, peer_slot],
            dst_ref=kv_all.at[b, s, peer_slot],
            send_sem=kv_send.at[b, s, j],
            recv_sem=kv_recv.at[b, s, lax.div(peer, 2)],
            device_id=(peer, c),
            device_id_type=MESH,
        )

    def twin_copy(b, s, half):
        blocks = pl.ds(half * COLS, COLS)
        return pltpu.make_async_remote_copy(
            src_ref=kv_all.at[b, s, blocks],
            dst_ref=kv_all.at[b, s, blocks],
            send_sem=twin_send.at[b, s],
            recv_sem=twin_recv.at[b, s],
            device_id=twin_id,
            device_id_type=MESH,
        )

    def part_copy(b, s, j):
        peer = lax.rem(c + j, COLS)
        return pltpu.make_async_remote_copy(
            src_ref=part.at[b, s, peer],
            dst_ref=part_in.at[b, s, c],
            send_sem=part_send.at[b, s, j],
            recv_sem=part_recv.at[b, s, c],
            device_id=(r, peer),
            device_id_type=MESH,
        )

    def part_arrival(b, s, j):
        peer = lax.rem(c + j, COLS)
        return pltpu.make_async_remote_copy(
            src_ref=part.at[b, s, peer],
            dst_ref=part_in.at[b, s, peer],
            send_sem=part_send.at[b, s, j],
            recv_sem=part_recv.at[b, s, peer],
            device_id=(r, peer),
            device_id_type=MESH,
        )

    def send_normed(b, s):
        q_all[b, s, c] = layer_norm(token_act[s]).astype(BF16)
        turn_copy(b, s).start()

    def send_queries(b, s):
        each(1, COLS, lambda j: q_copy(b, s, j).start())

    def pass_on(b, s):
        turn_arrival(b, s).wait_recv()
        each(1, ROWS // 2, lambda j: kv_copy(b, s, j).start())

    def gate(b, s):
        g = dot(q_all[b, s, c], proj[b, :, 3 * D_TOK :]).astype(BF16).astype(F32)
        gates[s] = 1.0 / (1.0 + jnp.exp(-g))

    def project_queries(b, s):
        each(1, COLS, lambda j: q_arrival(b, s, j).wait_recv())
        normed = q_all[b, s].reshape(QUERIES, D_TOK)
        for n in range(0, D_TOK, 256):
            q_ref[s, :, n : n + 256] = (
                dot(normed, proj[b, :, n : n + 256]) * (LOG2E / math.sqrt(HEAD))
            ).astype(BF16)

    def share(b, s):
        each(1, ROWS // 2, lambda j: kv_arrival(b, s, j).wait_recv())
        twin_copy(b, s, core).start()

    def project_keys(b, s, half):
        normed = kv_all[b, s, pl.ds(half * COLS, COLS)].reshape(KEYS // 2, D_TOK)
        rows = pl.ds(pl.multiple_of(half * (KEYS // 2), KEYS // 2), KEYS // 2)
        for n in range(0, D_TOK, 256):
            at = D_TOK + n
            k_ref[s, n : n + 256, rows] = dot(normed, proj[b, :, at : at + 256]).T.astype(BF16)
            at = 2 * D_TOK + n
            v_ref[s, rows, n : n + 256] = dot(normed, proj[b, :, at : at + 256]).astype(BF16)

    def attention(b, s):
        project_keys(b, s, core)
        twin_copy(b, s, 1 - core).wait_recv()
        project_keys(b, s, 1 - core)
        stat[...] = jnp.zeros_like(stat)
        lane = iota((QUERIES, C_ATOM), 1)

        def group(g, _):
            base = g * (8 * HEAD)
            outs = []
            stats = stat[...]
            for hh, (tile, tiles) in enumerate(HEAD_TILES):
                window = pl.ds(base + tile * 128, tiles * 128)
                at = iota((16, tiles * 128), 1) + tile * 128
                mine = jnp.where((at >= hh * HEAD) & (at < (hh + 1) * HEAD), 1.0, 0.0)
                query = q_ref[s, :, window].reshape(QUERIES // 16, 16, tiles * 128)
                query = (query * mine.astype(BF16)[None]).reshape(QUERIES, tiles * 128)
                rows = pl.ds((b * HEADS + g * 8 + hh) * STRIDE, QUERIES)
                score = dot(query, k_ref[s, window, :]) + jnp.concatenate(
                    [bias[t, rows, :] for t in range(KEYS // 128)], axis=1
                )
                top = jnp.max(score, axis=-1, keepdims=True)
                p = jnp.exp2(score - top)
                total = jnp.sum(p, axis=-1, keepdims=True)
                outs.append(dot(p.astype(BF16), v_ref[s, :, window]))
                stats = jnp.where(lane == g * 8 + hh, top, stats)
                stats = jnp.where(lane == HEADS + g * 8 + hh, total, stats)
            stat[...] = stats
            o0, o1, o2, o3, o4, o5, o6, o7 = outs
            tiles = (
                jnp.where(lane < 48, o0, jnp.where(lane < 96, o1, o2[:, :128])),
                jnp.where(
                    lane < 16,
                    o2[:, 128:],
                    jnp.where(lane < 64, o3, jnp.where(lane < 112, o4, o5[:, :128])),
                ),
                jnp.where(lane < 32, o5[:, 128:], jnp.where(lane < 80, o6, o7)),
            )
            for t, value in enumerate(tiles):
                where = pl.ds(base + t * 128, 128)
                part[b, s, :, :, where] = value.astype(BF16).reshape(COLS, TOK_DEV, 128)
            return 0

        group(0, 0)
        group(1, 0)
        exact = stat[...]
        high = exact.astype(BF16).astype(F32)
        rest = exact - high
        mid = rest.astype(BF16).astype(F32)
        pieces = high + pltpu.roll(mid, 32, 1) + pltpu.roll(rest - mid, 64, 1)
        part[b, s, :, :, D_TOK:PART] = pieces.astype(BF16).reshape(COLS, TOK_DEV, 128)
        each(1, COLS, lambda j: part_copy(b, s, j).start())
        part_in[b, s, c] = part[b, s, c]

    def combine(b, s):
        each(1, COLS, lambda j: part_arrival(b, s, j).wait_recv())
        pieces = part_in[b, s, :, :, D_TOK:PART].astype(F32).reshape(QUERIES, 128)
        stats = pieces + pltpu.roll(pieces, 96, 1) + pltpu.roll(pieces, 64, 1)
        stats = stats.reshape(COLS, TOK_DEV, 128)
        weight = jnp.exp2(stats - jnp.max(stats, axis=0, keepdims=True))
        dens = pltpu.roll(stats.reshape(QUERIES, 128), 128 - HEADS, 1).reshape(stats.shape)
        total = jnp.sum(weight * dens, axis=0, keepdims=True)
        weight = jnp.where(iota(stats.shape, 2) < HEADS, weight / total, 0.0)
        weight = weight.reshape(QUERIES, 128)
        high = weight.astype(BF16)
        low = (weight - high.astype(F32)).astype(BF16)
        spread = dot(jnp.concatenate([high, low], axis=1), expand[...], ((1,), (1,)))
        nums = part_in[b, s, :, :, 0:D_TOK].astype(F32)
        mix = jnp.sum(nums * spread.reshape(COLS, TOK_DEV, D_TOK), axis=0)
        gated = (gates[s] * mix).astype(BF16)
        token_act[s] = token_act[s] + dot(gated, tok_out[b])

    samples = range(SAMPLES)
    for s in samples:
        send_normed(0, s)
    for s in samples:
        send_queries(0, s)
    pair_bias(11, 16)
    for b in range(BLOCKS):
        for s in samples:
            pass_on(b, s)
        proj_copies[b].wait()
        for s in samples:
            gate(b, s)
        for s in samples:
            project_queries(b, s)
        for s in samples:
            share(b, s)
        for s in samples:
            attention(b, s)
        out_copies[b].wait()
        for s in samples:
            combine(b, s)
            if b + 1 < BLOCKS:
                send_normed(b + 1, s)
                send_queries(b + 1, s)

    for s in range(SAMPLES):
        dec_out[s] = dot(token_act[s].astype(BF16), w_dec[...])
    decoded = pltpu.make_async_remote_copy(
        src_ref=dec_out,
        dst_ref=dec_in,
        send_sem=dec_sems.at[0],
        recv_sem=dec_sems.at[1],
        device_id=up_id,
        device_id_type=MESH,
    )
    decoded.start()
    for b in range(BLOCKS):
        for s in range(SAMPLES):
            each(1, COLS, lambda j: q_copy(b, s, j).wait_send())
            turn_copy(b, s).wait_send()
            each(1, ROWS // 2, lambda j: kv_copy(b, s, j).wait_send())
            twin_copy(b, s, core).wait_send()
            each(1, COLS, lambda j: part_copy(b, s, j).wait_send())

    decoded.wait()
    member3 = jnp.concatenate([member_low] * 3, axis=0)
    for s in range(SAMPLES):
        table = jnp.concatenate([dec_in[s], dec_out[s]], axis=0)
        high = table.astype(BF16)
        rest = table - high.astype(F32)
        mid = rest.astype(BF16)
        low = (rest - mid.astype(F32)).astype(BF16)
        picked = dot(member3, jnp.concatenate([high, mid, low], axis=0), ((0,), (0,)))
        atom_dec = atom_enc[s * A_DEV : (s + 1) * A_DEV] + picked
        update = dot(w_update[...], layer_norm(atom_dec).astype(BF16), ((1,), (1,)))
        level = jnp.broadcast_to(noise_level[:, s : s + 1], (1, A_DEV))
        noisy = atom_pos[:, s] + level * noise[:, s]
        square = level * level + 1.0
        out[:, s] = noisy / square + level / jnp.sqrt(square) * update


def body(
    atom_pos,
    noise,
    noise_level,
    atom_single,
    w_pos,
    atom_bias,
    atom_qkv,
    atom_out,
    w_agg,
    atom_token,
    token_counts,
    pair,
    w_pairbias,
    tok_proj,
    tok_out,
    w_dec,
    w_update,
):
    vmem = pl.BlockSpec(memory_space=pltpu.VMEM)
    hbm = pl.BlockSpec(memory_space=pl.ANY)
    dma = pltpu.SemaphoreType.DMA
    denoised = pl.pallas_call(
        kernel,
        out_shape=jax.ShapeDtypeStruct((3, SAMPLES, A_DEV), F32),
        in_specs=[hbm] * 17,
        out_specs=vmem,
        scratch_shapes=[
            pltpu.VMEM((1, SAMPLES), F32),
            pltpu.VMEM((3, SAMPLES, A_DEV), F32),
            pltpu.VMEM((3, SAMPLES, A_DEV), F32),
            pltpu.VMEM((A_DEV, C_ATOM), BF16),
            pltpu.VMEM((3, C_ATOM), F32),
            pltpu.VMEM((HEADS_A, A_DEV, K_WIN), BF16),
            pltpu.VMEM((C_ATOM, 3 * C_ATOM), BF16),
            pltpu.VMEM((C_ATOM, C_ATOM), BF16),
            pltpu.VMEM((C_ATOM, D_TOK), BF16),
            pltpu.VMEM((1, A_DEV), jnp.int32),
            pltpu.VMEM((1, TOK_DEV), jnp.int32),
            pltpu.VMEM((2 * HEADS, C_ATOM), BF16),
            pltpu.VMEM((D_TOK, C_ATOM), BF16),
            pltpu.VMEM((3, C_ATOM), BF16),
            pltpu.VMEM((QUERIES, KEYS, C_ATOM), BF16),
            pltpu.VMEM((BLOCKS, D_TOK, 4 * D_TOK), BF16),
            pltpu.VMEM((BLOCKS, D_TOK, D_TOK), BF16),
            pltpu.VMEM((KEYS // 128, 2 * HEADS * STRIDE, 128), F32),
            pltpu.VMEM((8 * C_ATOM, KEYS), BF16),
            pltpu.VMEM((KEYS, KEYS), BF16),
            pltpu.VMEM((D_TOK, 2 * C_ATOM), BF16),
            pltpu.VMEM((SAMPLES * A_DEV, C_ATOM), F32),
            pltpu.VMEM((SAMPLES, A_DEV, C_ATOM), BF16),
            pltpu.VMEM((SAMPLES, A_DEV, 2 * C_ATOM), BF16),
            pltpu.VMEM((2, SAMPLES, MARGIN, 2 * C_ATOM), BF16),
            pltpu.VMEM((SAMPLES, A_DEV + 2 * MARGIN, 2 * C_ATOM), BF16),
            pltpu.VMEM((SAMPLES, TOK_DEV, D_TOK), BF16),
            pltpu.VMEM((SAMPLES, TOK_DEV, D_TOK), BF16),
            pltpu.VMEM((SAMPLES, TOK_DEV, D_TOK), F32),
            pltpu.VMEM((SAMPLES, TOK_DEV, D_TOK), F32),
            pltpu.VMEM((BLOCKS, SAMPLES, COLS, TOK_DEV, D_TOK), BF16),
            pltpu.VMEM((BLOCKS, SAMPLES, ROWS, TOK_DEV, D_TOK), BF16),
            pltpu.VMEM((SAMPLES, QUERIES, D_TOK), BF16),
            pltpu.VMEM((SAMPLES, D_TOK, KEYS), BF16),
            pltpu.VMEM((SAMPLES, KEYS, D_TOK), BF16),
            pltpu.VMEM((QUERIES, 128), F32),
            pltpu.VMEM((BLOCKS, SAMPLES, COLS, TOK_DEV, PART), BF16),
            pltpu.VMEM((BLOCKS, SAMPLES, COLS, TOK_DEV, PART), BF16),
            pltpu.VMEM((SAMPLES, TOK_DEV, C_ATOM), F32),
            pltpu.VMEM((SAMPLES, TOK_DEV, C_ATOM), F32),
            dma((14,)),
            dma((4,)),
            dma((4,)),
            dma((2,)),
            dma((2,)),
            dma((2,)),
            dma((2,)),
            dma((BLOCKS, SAMPLES)),
            dma((BLOCKS, SAMPLES)),
            dma((BLOCKS, SAMPLES, COLS)),
            dma((BLOCKS, SAMPLES, COLS)),
            dma((BLOCKS, SAMPLES, ROWS // 2)),
            dma((BLOCKS, SAMPLES, ROWS // 2)),
            dma((BLOCKS, SAMPLES)),
            dma((BLOCKS, SAMPLES)),
            dma((BLOCKS, SAMPLES, COLS)),
            dma((BLOCKS, SAMPLES, COLS)),
        ],
        compiler_params=pltpu.CompilerParams(
            collective_id=0, has_side_effects=True, vmem_limit_bytes=56 * 1024 * 1024
        ),
    )(
        noise_level.reshape(1, SAMPLES),
        atom_pos.transpose(1, 0, 2),
        noise.transpose(1, 0, 2),
        atom_single,
        w_pos,
        atom_bias,
        atom_qkv,
        atom_out,
        w_agg,
        atom_token.reshape(1, A_DEV),
        token_counts.reshape(1, TOK_DEV),
        pair,
        w_pairbias.T,
        tok_proj,
        tok_out,
        w_dec,
        w_update.T,
    )
    return denoised.transpose(1, 0, 2)


def solution(mesh):
    return jax.shard_map(
        body,
        mesh=mesh,
        in_specs=(
            P(None, None, ("row", "col")),
            P(None, None, ("row", "col")),
            P(),
            P(("row", "col"), None),
            P(),
            P(None, ("row", "col"), None),
            P(),
            P(),
            P(),
            P(("row", "col")),
            P(("row", "col")),
            P("row", "col", None),
            P(),
            P(),
            P(),
            P(),
            P(),
        ),
        out_specs=P(None, None, ("row", "col")),
        check_vma=False,
    )
```

profile of v0, /device:TPU:1, one launch (start us, length us, event | category | flops | bytes accessed | tf_op | source)
XLA Modules:
  0.0 75.8 jit_solution(694707324490231188)
XLA Ops:
  0.0 74.5 %shard_map.163 = f32[3,2,128]{2,1,0:T(2,128)} custom-call(f32[1,2]{1,0:T(1,128)} %bitcast.13, f32[3,2,128]{2,1,0:T(2,128)} %bitcast.10, f32[3,2,128]{2,1,0:T(2,128)} %bitcast.11, bf16[128,128]{1,0:T(8,128)(2,1)} %atom_single_hbm.1, f32[3,128]{1,0:T(4,128)} %w_pos_hbm.1, bf16[4,128,128]{2,1,0:T(8,128)(2,1)} %atom_bias_hbm.1, bf16[128,384]{1,0:T(8,128)(2,1)} %atom_qkv_hbm.1, ...), custom_call_target="tpu_custom_call" | custom-call | tf_op jit(solution)/shard_map/pallas_call | solution.py:656
  74.5 1.3 %copy.19 = f32[2,3,128]{2,0,1:T(2,128)} copy(f32[2,3,128]{2,0,1:T(2,128)} %bitcast.8) | data formatting | bytes 6144
where the time goes:
time: 75.9 us; the launch traced here: 75.8 us
  Pallas kernels  74.5 us (98%)
  local copies, waits for them, and re-layouts  1.26 us (2%)
    pallas_call x1, Pallas kernels, body(): pl.pallas_call(kernel, out_shape=jax.ShapeDtypeStruct((3, SAMPLES, A_DEV)...  74.5 us

commit v1 on v0

--- a/solution.py
+++ b/solution.py
@@ -306,26 +306,30 @@
     head_mask = jnp.where(lane_head, 1.0, 0.0)
     head_mask_low = head_mask.astype(BF16)
     slots = iota((1, K_WIN), 1)
-    for s in range(SAMPLES):
-        mixed = []
-        for w in range(A_DEV // Q_WIN):
-            rows = slice(w * Q_WIN, (w + 1) * Q_WIN)
-            window = slice(w * Q_WIN, w * Q_WIN + K_WIN)
-            query = (queries_a[s, rows][None] * head_mask_low).reshape(HEADS_A * Q_WIN, C_ATOM)
-            score = dot(query, kv_pad[s, window, 0:C_ATOM], ((1,), (1,))) * (1 / math.sqrt(HEAD_A))
-            score = score + atom_bias[:, rows, :].astype(F32).reshape(HEADS_A * Q_WIN, K_WIN)
-            index = d * A_DEV + w * Q_WIN - MARGIN + slots
-            inside = (index >= 0) & (index < DEVICES * A_DEV)
-            score = jnp.where(inside, score, -1e30)
-            p = jnp.exp(score - jnp.max(score, axis=-1, keepdims=True))
-            total = jnp.sum(p, axis=-1, keepdims=True)
-            mix = dot(p.astype(BF16), kv_pad[s, window, C_ATOM:]) / total
-            mixed.append(
-                jnp.sum(mix.reshape(HEADS_A, Q_WIN, C_ATOM) * head_mask, axis=0)
-            )
-        rows = slice(s * A_DEV, (s + 1) * A_DEV)
-        mix = jnp.concatenate(mixed, axis=0).astype(BF16)
-        atom_enc[rows] = atom_enc[rows] + dot(mix, atom_out[...])
+    windows = [(s, w) for s in range(SAMPLES) for w in range(A_DEV // Q_WIN)]
+    scores = []
+    for s, w in windows:
+        rows = slice(w * Q_WIN, (w + 1) * Q_WIN)
+        keys = kv_pad[s, w * Q_WIN : w * Q_WIN + K_WIN, 0:C_ATOM]
+        query = (queries_a[s, rows][None] * head_mask_low).reshape(HEADS_A * Q_WIN, C_ATOM)
+        scores.append(dot(query, keys, ((1,), (1,))))
+    weights = []
+    for (s, w), score in zip(windows, scores):
+        rows = slice(w * Q_WIN, (w + 1) * Q_WIN)
+        score = score * (1 / math.sqrt(HEAD_A))
+        score = score + atom_bias[:, rows, :].astype(F32).reshape(HEADS_A * Q_WIN, K_WIN)
+        index = d * A_DEV + w * Q_WIN - MARGIN + slots
+        inside = (index >= 0) & (index < DEVICES * A_DEV)
+        score = jnp.where(inside, score, -1e30)
+        p = jnp.exp(score - jnp.max(score, axis=-1, keepdims=True))
+        weights.append((p.astype(BF16), jnp.sum(p, axis=-1, keepdims=True)))
+    mixed = []
+    for (s, w), (p, total) in zip(windows, weights):
+        mix = dot(p, kv_pad[s, w * Q_WIN : w * Q_WIN + K_WIN, C_ATOM:]) / total
+        mixed.append(jnp.sum(mix.reshape(HEADS_A, Q_WIN, C_ATOM) * head_mask, axis=0))
+    atom_enc[...] = atom_enc[...] + dot(
+        jnp.concatenate(mixed, axis=0).astype(BF16), atom_out[...]
+    )
 
     slot_index = atom_token[...] - (d * TOK_DEV - TOK_DEV)
     member = jnp.where(

time: 75.9 us -> 74.8 us (0.986)
  Pallas kernels: 74.5 us -> 73.4 us
    pallas_call x1, Pallas kernels: 74.5 us -> 73.4 us  [body(): pl.pallas_call(kernel, out_shape=jax.ShapeDtypeStruct((3, SAMPLES, A_DEV)...]
where the time goes in v1:
time: 74.8 us; the launch traced here: 74.6 us
  Pallas kernels  73.4 us (98%)
  local copies, waits for them, and re-layouts  1.26 us (2%)
    pallas_call x1, Pallas kernels, body(): pl.pallas_call(kernel, out_shape=jax.ShapeDtypeStruct((3, SAMPLES, A_DEV)...  73.4 us

profile of v1, /device:TPU:1, one launch (start us, length us, event | category | flops | bytes accessed | tf_op | source)
XLA Modules:
  0.0 74.6 jit_solution(6372818816295503454)
XLA Ops:
  0.0 73.4 %shard_map.163 = f32[3,2,128]{2,1,0:T(2,128)} custom-call(f32[1,2]{1,0:T(1,128)} %bitcast.13, f32[3,2,128]{2,1,0:T(2,128)} %bitcast.10, f32[3,2,128]{2,1,0:T(2,128)} %bitcast.11, bf16[128,128]{1,0:T(8,128)(2,1)} %atom_single_hbm.1, f32[3,128]{1,0:T(4,128)} %w_pos_hbm.1, bf16[4,128,128]{2,1,0:T(8,128)(2,1)} %atom_bias_hbm.1, bf16[128,384]{1,0:T(8,128)(2,1)} %atom_qkv_hbm.1, ...), custom_call_target="tpu_custom_call" | custom-call | tf_op jit(solution)/shard_map/pallas_call | solution.py:660
  73.4 1.3 %copy.19 = f32[2,3,128]{2,0,1:T(2,128)} copy(f32[2,3,128]{2,0,1:T(2,128)} %bitcast.8) | data formatting | bytes 6144

commit v2 on v1

--- a/solution.py
+++ b/solution.py
@@ -471,11 +471,11 @@
         turn_copy(b, s).start()
 
     def send_queries(b, s):
-        each(1, COLS, lambda j: q_copy(b, s, j).start())
+        each(0, COLS - 1, lambda j: q_copy(b, s, COLS - 1 - j).start())
 
     def pass_on(b, s):
         turn_arrival(b, s).wait_recv()
-        each(1, ROWS // 2, lambda j: kv_copy(b, s, j).start())
+        each(0, ROWS // 2 - 1, lambda j: kv_copy(b, s, ROWS // 2 - 1 - j).start())
 
     def gate(b, s):
         g = dot(q_all[b, s, c], proj[b, :, 3 * D_TOK :]).astype(BF16).astype(F32)
@@ -553,7 +553,7 @@
         mid = rest.astype(BF16).astype(F32)
         pieces = high + pltpu.roll(mid, 32, 1) + pltpu.roll(rest - mid, 64, 1)
         part[b, s, :, :, D_TOK:PART] = pieces.astype(BF16).reshape(COLS, TOK_DEV, 128)
-        each(1, COLS, lambda j: part_copy(b, s, j).start())
+        each(0, COLS - 1, lambda j: part_copy(b, s, COLS - 1 - j).start())
         part_in[b, s, c] = part[b, s, c]
 
     def combine(b, s):

time: 74.8 us -> 75.9 us (1.015)
  Pallas kernels: 73.4 us -> 74.5 us
    pallas_call x1, Pallas kernels: 73.4 us -> 74.5 us  [body(): pl.pallas_call(kernel, out_shape=jax.ShapeDtypeStruct((3, SAMPLES, A_DEV)...]
where the time goes in v2:
time: 75.9 us; the launch traced here: 75.8 us
  Pallas kernels  74.5 us (98%)
  local copies, waits for them, and re-layouts  1.26 us (2%)
    pallas_call x1, Pallas kernels, body(): pl.pallas_call(kernel, out_shape=jax.ShapeDtypeStruct((3, SAMPLES, A_DEV)...  74.5 us

profile of v2, /device:TPU:1, one launch (start us, length us, event | category | flops | bytes accessed | tf_op | source)
XLA Modules:
  0.0 75.8 jit_solution(3480859717198036146)
XLA Ops:
  0.0 74.5 %shard_map.163 = f32[3,2,128]{2,1,0:T(2,128)} custom-call(f32[1,2]{1,0:T(1,128)} %bitcast.13, f32[3,2,128]{2,1,0:T(2,128)} %bitcast.10, f32[3,2,128]{2,1,0:T(2,128)} %bitcast.11, bf16[128,128]{1,0:T(8,128)(2,1)} %atom_single_hbm.1, f32[3,128]{1,0:T(4,128)} %w_pos_hbm.1, bf16[4,128,128]{2,1,0:T(8,128)(2,1)} %atom_bias_hbm.1, bf16[128,384]{1,0:T(8,128)(2,1)} %atom_qkv_hbm.1, ...), custom_call_target="tpu_custom_call" | custom-call | tf_op jit(solution)/shard_map/pallas_call | solution.py:660
  74.5 1.3 %copy.19 = f32[2,3,128]{2,0,1:T(2,128)} copy(f32[2,3,128]{2,0,1:T(2,128)} %bitcast.8) | data formatting | bytes 6144
